TPU v7x, 128 devices: a whole 4x4x4 slice. The times are simulated.
128 devices in a mesh: dp: 4 (over x), frame: 4 (over z), expert: 8 (over y, core).
Axes of the slice: x: 4, y: 4, z: 4, core: 2. Of those that a mesh axis runs over, the one named last changes fastest.
Arguments:
- queries: bfloat16 [16384, 2048], P(('dp', 'frame'), 'expert'), parts along dimension 0, may hold values from -8 to 8
- keys: bfloat16 [16384, 2048], P(('dp', 'frame'), 'expert'), parts along dimension 0, may hold values from -8 to 8
- values: bfloat16 [16384, 2048], P(('dp', 'frame'), 'expert'), parts along dimension 0, may hold values from -6 to 6
- hidden_state: bfloat16 [16384, 4096], P(('dp', 'frame', 'expert')), parts along dimension 0, may hold values from -60 to 60
- out_grad: bfloat16 [16384, 4096], P(('dp', 'frame', 'expert')), parts along dimension 0, may hold values from -6 to 6
- stored_pre: bfloat16 [16384, 2, 2, 2048], P(('dp', 'frame', 'expert')), parts along dimension 0, may hold values from -6 to 6
- expert_ids: int32 [16384, 2], P(('dp', 'frame', 'expert')), parts along dimension 0, may hold values from 0 to 7, as said below
- gate_weights: float32 [16384, 2], P(('dp', 'frame', 'expert')), parts along dimension 0, may hold values from 0.25 to 1
- w_gate: bfloat16 [8, 4096, 2048], P('expert', None, 'frame'), may hold values from -0.09375 to 0.09375
- w_up: bfloat16 [8, 4096, 2048], P('expert', None, 'frame'), may hold values from -0.09375 to 0.09375
- w_down: bfloat16 [8, 2048, 4096], P('expert', 'frame'), may hold values from -0.125 to 0.125
Outputs:
- residual_grad: bfloat16 [16384, 4096], P(('dp', 'frame', 'expert')), parts along dimension 0
- query_grad: bfloat16 [16384, 2048], P(('dp', 'frame'), 'expert'), parts along dimension 0
- key_grad: bfloat16 [16384, 2048], P(('dp', 'frame'), 'expert'), parts along dimension 0
- value_grad: bfloat16 [16384, 2048], P(('dp', 'frame'), 'expert'), parts along dimension 0
There are 4 independent parts, one for each index of `dp`. A program takes and returns all parts, laid end to end along the dimension named above; an argument that names none is the same for every part. Nothing has to cross between parts.
Inputs may be any that keep to these rules, and one draw needn't show every extreme that they name: `expert_ids`: each token names 2 different experts. In the tokens of one device (aligned blocks of 128 rows) no expert is named more than 36 times; in each span one expert is named exactly 36 times in every block of that span.
All inputs are finite; a program needn't handle non-finite values.
Results may differ from a plain program's by a relative error of at most 0.015.
Values may be sent and summed in bfloat16 or wider, within the bound.
A program may use at most 192 MiB of HBM per device.

v0:
```python
import jax
import jax.numpy as jnp
from jax import lax
from jax.sharding import PartitionSpec as P

HD = 128
CAP = 36


masked_score = -1e30


def hidden_grads(routed_rows, stored_rows, down_weight):
    hidden = jnp.einsum(
        "...lcd,lhd->...lch", routed_rows, down_weight, preferred_element_type=jnp.float32
    )
    gate_value = stored_rows[..., 0, :].astype(jnp.float32)
    up_value = stored_rows[..., 1, :].astype(jnp.float32)
    gate_sigmoid = jax.nn.sigmoid(gate_value)
    gate_grad = (
        hidden * up_value * gate_sigmoid * (1.0 + gate_value * (1.0 - gate_sigmoid))
    ).astype(jnp.bfloat16)
    up_grad = (hidden * gate_value * gate_sigmoid).astype(jnp.bfloat16)
    return jnp.stack([gate_grad, up_grad], axis=-2)


def input_terms(grad_rows, gate_weight, up_weight):
    term = jnp.einsum(
        "...lch,ldh->...lcd", grad_rows[..., 0, :], gate_weight, preferred_element_type=jnp.float32
    )
    return term + jnp.einsum(
        "...lch,ldh->...lcd", grad_rows[..., 1, :], up_weight, preferred_element_type=jnp.float32
    )


def head_backward(query_rows, key_rows, value_rows, grad_rows, allowed):
    score_scale = HD ** (-0.5)
    scores = (
        jnp.einsum("qd,kd->qk", query_rows, key_rows, preferred_element_type=jnp.float32)
        * score_scale
    )
    scores = jnp.where(allowed, scores, masked_score)
    largest = jnp.max(scores, axis=-1, keepdims=True)
    exponent = jnp.exp(scores - largest)
    softmax = exponent / jnp.sum(exponent, axis=-1, keepdims=True)
    softmax_grad = jnp.einsum(
        "qd,kd->qk", grad_rows, value_rows, preferred_element_type=jnp.float32
    )
    centre = jnp.sum(softmax * softmax_grad, axis=-1, keepdims=True)
    score_grads = (softmax * (softmax_grad - centre) * score_scale).astype(jnp.bfloat16)
    softmax_low = softmax.astype(jnp.bfloat16)
    query_part = jnp.einsum("qk,kd->qd", score_grads, key_rows, preferred_element_type=jnp.float32)
    key_part = jnp.einsum("qk,qd->kd", score_grads, query_rows, preferred_element_type=jnp.float32)
    value_part = jnp.einsum("qk,qd->kd", softmax_low, grad_rows, preferred_element_type=jnp.float32)
    return (query_part.astype(jnp.bfloat16), key_part, value_part)


def split_heads(matrix):
    head_count = matrix.shape[1] // HD
    return matrix.reshape(matrix.shape[0], head_count, HD).transpose(1, 0, 2)


def join_heads(stacked):
    return stacked.transpose(1, 0, 2).reshape(stacked.shape[1], stacked.shape[0] * HD)


def heads_backward(query_block, key_block, value_block, grad_block, allowed):

    def one_head(operands):
        return head_backward(operands[0], operands[1], operands[2], operands[3], allowed)

    results = lax.map(
        one_head,
        (
            split_heads(query_block),
            split_heads(key_block),
            split_heads(value_block),
            split_heads(grad_block),
        ),
    )
    return (join_heads(results[0]), join_heads(results[1]), join_heads(results[2]))


def on_device(
    queries,
    keys,
    values,
    hidden_state,
    out_grad,
    stored_pre,
    expert_ids,
    gate_weights,
    w_gate,
    w_up,
    w_down,
):
    tok_rows, model_width = out_grad.shape
    top_count = expert_ids.shape[1]
    local_experts = w_gate.shape[0]
    ff_local = w_gate.shape[2]
    expert_count = lax.axis_size("expert")
    frame_count = lax.axis_size("frame")
    all_experts = local_experts * expert_count
    pair_count = tok_rows * top_count
    flat_ids = expert_ids.reshape(pair_count)
    expert_hits = (flat_ids[:, None] == jnp.arange(all_experts, dtype=jnp.int32)[None, :]).astype(
        jnp.int32
    )
    earlier = jnp.cumsum(expert_hits, axis=0) - expert_hits
    slot_index = jnp.sum(earlier * expert_hits, axis=1)
    target_slot = flat_ids * CAP + slot_index
    route_table = (
        target_slot[:, None] == jnp.arange(all_experts * CAP, dtype=jnp.int32)[None, :]
    ).astype(jnp.bfloat16)
    pair_grad = (
        (gate_weights[:, :, None] * out_grad[:, None, :].astype(jnp.float32))
        .astype(jnp.bfloat16)
        .reshape(pair_count, model_width)
    )
    send_rows = jnp.einsum(
        "ps,pd->sd", route_table, pair_grad, preferred_element_type=jnp.float32
    ).astype(jnp.bfloat16)
    send_rows = send_rows.reshape(expert_count, local_experts, CAP, model_width)
    stored_groups = stored_pre.reshape(pair_count, 2, frame_count, ff_local)
    send_stored = jnp.einsum(
        "ps,pkfh->fskh", route_table, stored_groups, preferred_element_type=jnp.float32
    ).astype(jnp.bfloat16)
    send_stored = send_stored.reshape(frame_count, expert_count, local_experts, CAP, 2 * ff_local)
    row_copies = jnp.broadcast_to(send_rows[None], (frame_count,) + send_rows.shape)
    rows_all, stored_all = (
        lax.all_to_all(
            row_copies.reshape(frame_count * expert_count, local_experts, CAP, model_width),
            ("frame", "expert"),
            split_axis=0,
            concat_axis=0,
            tiled=True,
        ),
        lax.all_to_all(
            send_stored.reshape(frame_count * expert_count, local_experts, CAP, 2 * ff_local),
            ("frame", "expert"),
            split_axis=0,
            concat_axis=0,
            tiled=True,
        ),
    )
    rows_all = rows_all.reshape(frame_count, expert_count, local_experts, CAP, model_width)
    stored_all = stored_all.reshape(frame_count, expert_count, local_experts, CAP, 2, ff_local)
    grads_all = hidden_grads(rows_all, stored_all, w_down)
    term_low = input_terms(grads_all, w_gate, w_up).astype(jnp.bfloat16)
    partial_back = lax.all_to_all(
        term_low.reshape(frame_count * expert_count, local_experts, CAP, model_width),
        ("frame", "expert"),
        split_axis=0,
        concat_axis=0,
        tiled=True,
    )
    summed = jnp.sum(
        partial_back.reshape(frame_count, all_experts * CAP, model_width).astype(jnp.float32),
        axis=0,
    )
    returned = summed.astype(jnp.bfloat16)
    pair_input = jnp.einsum("ps,sd->pd", route_table, returned, preferred_element_type=jnp.float32)
    moe_grad = jnp.sum(pair_input.reshape(tok_rows, top_count, model_width), axis=1)
    state = hidden_state.astype(jnp.float32)
    inverse_rms = lax.rsqrt(jnp.mean(state * state, axis=-1, keepdims=True) + 1e-06)
    normed = state * inverse_rms
    residual = out_grad.astype(jnp.float32) + inverse_rms * (
        moe_grad - normed * jnp.mean(moe_grad * normed, axis=-1, keepdims=True)
    )
    residual_grad = residual.astype(jnp.bfloat16)
    att_local = queries.shape[1]
    span_rows = queries.shape[0]
    grad_local = lax.all_to_all(
        residual_grad[:, : att_local * expert_count],
        "expert",
        split_axis=1,
        concat_axis=0,
        tiled=True,
    )
    key_all, value_all = (
        lax.all_gather(keys, "frame", axis=0, tiled=True),
        lax.all_gather(values, "frame", axis=0, tiled=True),
    )
    frame_index = lax.axis_index("frame")
    key_span = jnp.arange(key_all.shape[0], dtype=jnp.int32) // span_rows
    allowed = (key_span <= frame_index)[None, :]
    query_grad, key_part, value_part = heads_backward(
        queries, key_all, value_all, grad_local, allowed
    )
    key_sum, value_sum = (
        lax.psum_scatter(
            key_part.astype(jnp.bfloat16), "frame", scatter_dimension=0, tiled=True
        ).astype(jnp.float32),
        lax.psum_scatter(
            value_part.astype(jnp.bfloat16), "frame", scatter_dimension=0, tiled=True
        ).astype(jnp.float32),
    )
    key_grad = key_sum.astype(jnp.bfloat16)
    value_grad = value_sum.astype(jnp.bfloat16)
    return (residual_grad, query_grad, key_grad, value_grad)


def solution(mesh):
    return jax.shard_map(
        on_device,
        mesh=mesh,
        in_specs=(
            P(("dp", "frame"), "expert"),
            P(("dp", "frame"), "expert"),
            P(("dp", "frame"), "expert"),
            P(("dp", "frame", "expert"), None),
            P(("dp", "frame", "expert"), None),
            P(("dp", "frame", "expert"), None, None, None),
            P(("dp", "frame", "expert"), None),
            P(("dp", "frame", "expert"), None),
            P("expert", None, "frame"),
            P("expert", None, "frame"),
            P("expert", "frame", None),
        ),
        out_specs=(
            P(("dp", "frame", "expert"), None),
            P(("dp", "frame"), "expert"),
            P(("dp", "frame"), "expert"),
            P(("dp", "frame"), "expert"),
        ),
        check_vma=False,
    )
```

profile of v0, /device:TPU:1, one launch (start us, length us, event | category | flops | bytes accessed | tf_op | source)
XLA Modules:
  0.0 583.5 jit_solution(10770194959237435)
XLA Ops:
  19.3 9.8 %all-to-all-start.1 = ((bf16[32,1,36,1024]{3,2,1,0:T(8,128)(2,1)}), bf16[32,1,36,1024]{3,2,1,0:T(8,128)(2,1)}, u32[]{:S(2)}, u32[]{:S(2)}) async-start(bf16[32,1,36,1024]{3,2,1,0:T(8,128)(2,1)} %bitcast.13), calls=%async_computation.1 | async-start | bytes 5242880 | tf_op jit(solution)/shard_map/all_to_all | solution.py:138
  29.1 4.0 mul.111
  33.2 6.1 %mul.112 = f32[256,4096]{1,0:T(8,128)} reshape(f32[128,2,4096]{2,1,0:T(2,128)} %mul.111) | data formatting | bytes 8388608 | tf_op jit(solution)/shard_map/mul | solution.py:116
  44.8 17.9 %all-to-all-done.1 = bf16[32,1,36,1024]{3,2,1,0:T(8,128)(2,1)} async-done(((bf16[32,1,36,1024]{3,2,1,0:T(8,128)(2,1)}), bf16[32,1,36,1024]{3,2,1,0:T(8,128)(2,1)}, u32[]{:S(2)}, u32[]{:S(2)}) %all-to-all-start.1) | async-done | bytes 2359328 | tf_op jit(solution)/shard_map/all_to_all | solution.py:138
  62.7 7.1 %broadcast_in_dim.49 = bf16[4,8,36,4096]{3,2,1,0:T(8,128)(2,1)} broadcast(bf16[8,36,4096]{2,1,0:T(8,128)(2,1)} %broadcast_in_dim.48), dimensions={1,2,3} | broadcast | bytes 11796480 | tf_op jit(solution)/shard_map/broadcast_in_dim | solution.py:129
  69.8 7.7 %all-to-all-start = ((bf16[32,1,36,4096]{3,2,1,0:T(8,128)(2,1)}), bf16[32,1,36,4096]{3,2,1,0:T(8,128)(2,1)}, u32[]{:S(2)}, u32[]{:S(2)}) async-start(bf16[32,1,36,4096]{3,2,1,0:T(8,128)(2,1)} %bitcast.200), calls=%async_computation | async-start | bytes 20971520 | tf_op jit(solution)/shard_map/all_to_all | solution.py:131
  77.5 5.7 reshape.258
  83.2 5.5 fusion.85
  88.7 114.6 %all-to-all-done = bf16[32,1,36,4096]{3,2,1,0:T(8,128)(2,1)} async-done(((bf16[32,1,36,4096]{3,2,1,0:T(8,128)(2,1)}), bf16[32,1,36,4096]{3,2,1,0:T(8,128)(2,1)}, u32[]{:S(2)}, u32[]{:S(2)}) %all-to-all-start) | async-done | bytes 9437216 | tf_op jit(solution)/shard_map/all_to_all | solution.py:131
  203.3 9.7 %fusion.38 = f32[4,8,36,512]{3,2,1,0:T(8,128)S(1)} fusion(bf16[1,512,4096]{2,1,0:T(8,128)(2,1)} %param.23, bf16[4,8,36,4096]{3,2,1,0:T(8,128)(2,1)} %bitcast.175), kind=kOutput, calls=%fused_computation.44 | convolution fusion | flops 4831838208 | bytes 15990784 | tf_op jit(solution)/shard_map/...lcd,lhd->...lch/dot_general | solution.py:14
  214.5 11.0 %fusion.41 = f32[4,8,36,4096]{3,2,1,0:T(8,128)} fusion(bf16[1,4096,512]{2,1,0:T(8,128)(2,1)S(1)} %copy-done.15, f32[4,8,36,512]{3,2,1,0:T(8,128)S(1)} %fusion.38, bf16[4,8,1,36,1,512]{5,4,3,1,0,2:T(2,128)(2,1)S(1)} %copy-done.5, bf16[4,8,1,36,1,512]{5,4,3,1,0,2:T(2,128)(2,1)S(1)} %copy-done.4), kind=kOutput, calls=%fused_computation.48 | convolution fusion | flops 4838916096 | bytes 27787264 | tf_op jit(solution)/shard_map/...lch,ldh->...lcd/dot_general | solution.py:28
  225.4 14.7 %add_convert_fusion = bf16[4,8,36,4096]{3,2,1,0:T(8,128)(2,1)} fusion(f32[4,8,36,4096]{3,2,1,0:T(8,128)} %fusion.41, bf16[1,4096,512]{2,1,0:T(8,128)(2,1)} %param.22, f32[4,8,36,512]{3,2,1,0:T(8,128)} %copy-done.17, bf16[4,8,1,36,1,512]{5,4,3,1,0,2:T(2,128)(2,1)S(1)} %copy-done.4), kind=kOutput, calls=%fused_computation.43 | convolution fusion | flops 4845404160 | bytes 36044800 | tf_op jit(solution)/shard_map/...lch,ldh->...lcd/dot_general | solution.py:31
  240.1 11.8 %all-to-all-start.2 = ((bf16[32,1,36,4096]{3,2,1,0:T(8,128)(2,1)}), bf16[32,1,36,4096]{3,2,1,0:T(8,128)(2,1)}, u32[]{:S(2)}, u32[]{:S(2)}) async-start(bf16[32,1,36,4096]{3,2,1,0:T(8,128)(2,1)} %bitcast.203), calls=%async_computation.2 | async-start | bytes 20971520 | tf_op jit(solution)/shard_map/all_to_all | solution.py:150
  254.7 133.4 %all-to-all-done.2 = bf16[32,1,36,4096]{3,2,1,0:T(8,128)(2,1)} async-done(((bf16[32,1,36,4096]{3,2,1,0:T(8,128)(2,1)}), bf16[32,1,36,4096]{3,2,1,0:T(8,128)(2,1)}, u32[]{:S(2)}, u32[]{:S(2)}) %all-to-all-start.2) | async-done | bytes 9437216 | tf_op jit(solution)/shard_map/all_to_all | solution.py:150
  388.1 13.3 %reshape.245 = bf16[4,288,4096]{2,1,0:T(8,128)(2,1)} reshape(bf16[32,1,36,4096]{3,2,1,0:T(8,128)(2,1)} %all-to-all-done.2) | data formatting | bytes 18874368 | tf_op jit(solution)/shard_map/reshape | solution.py:158
  401.4 5.7 reduce_sum.71
  412.4 4.4 all-to-all-start.3
  417.0 9.3 %all-to-all-done.3 = bf16[128,8,256]{0,2,1:T(8,128)(2,1)S(1)} async-done(((bf16[128,8,256]{0,2,1:T(8,128)(2,1)}), bf16[128,8,256]{0,2,1:T(8,128)(2,1)S(1)}, u32[]{:S(2)}, u32[]{:S(2)}) %all-to-all-start.3) | async-done | bytes 524320 | tf_op jit(solution)/shard_map/all_to_all | solution.py:173
  427.7 86.1 %while.15 = (s32[]{:T(128)}, bf16[2,1024,128]{2,1,0:T(8,128)(2,1)}, bf16[2,4096,128]{2,1,0:T(8,128)(2,1)}, bf16[2,4096,128]{2,1,0:T(8,128)(2,1)}, bf16[2,1024,12...) while((s32[]{:T(128)}, bf16[2,1024,128]{2,1,0:T(8,128)(2,1)}, ...), condition=%wide.region_11.12_spmd.clone, body=%wide.region_7.11_spmd.clone.sunk | while | flops 5477925888 | bytes 172303584 | solution.py:72
  427.9 4.0 fusion.108
  431.9 4.3 fusion.109
  436.2 7.7 %fusion.112 = bf16[2,4096,128]{2,1,0:T(8,128)(2,1)} fusion(bf16[2,4096,128]{2,1,0:T(8,128)(2,1)} %get-tuple-element.204, s32[]{:T(128)} %get-tuple-element.201, bf16[2,1024,128]{1,2,0:T(8,128)(2,1)} %get-tuple-element.217, f32[1024,4096]{1,0:T(8,128)S(1)} %get-tuple-element.187, f32[1024]{0:T(1024)S(1)} %fusion.109, ...), kind=kOutput, calls=%fused_computation.11.clone.1 | convolution fusion | flops 1094713344 | bytes 19149824 | tf_op jit(solution)/shard_map/while/body/eval_jaxpr/qk,qd->kd/dot_general | solution.py:54
  443.9 9.9 %multiply_reduce_fusion.2 = (f32[1024]{0:T(1024)S(1)}, f32[1024,4096]{1,0:T(8,128)}) fusion(f32[1024]{0:T(1024)S(1)} %fusion.109, f32[1024]{0:T(1024)S(1)} %get-tuple-element.188, f32[1024,4096]{1,0:T(8,128)S(1)} %get-tuple-element.187, pred[4096]{0:T(1024)(128)(4,1)S(1)} %compare_reduce_fusion.2, bf16[2,4096,128]{1,2,0:T(8,128)(2,1)S(1)} %copy-done.16, ...), kind=kOutput, calls=%fused_computation.2.clone.1 | convolution fusion | flops 1098906624 | bytes 34882560 | tf_op jit(solution)/shard_map/while/body/eval_jaxpr/qd,kd->qk/dot_general | solution.py:46
  453.8 10.2 %multiply_convert_fusion.4 = bf16[1024,4096]{1,0:T(8,128)(2,1)S(1)} fusion(f32[1024,4096]{1,0:T(8,128)} %get-tuple-element.189, f32[1024]{0:T(1024)S(1)} %get-tuple-element.190, f32[1024]{0:T(1024)S(1)} %fusion.109, f32[1024]{0:T(1024)S(1)} %get-tuple-element.188, f32[1024,4096]{1,0:T(8,128)S(1)} %get-tuple-element.187, ...), kind=kLoop, calls=%fused_computation.1.clone.1 | loop fusion | flops 33554432 | bytes 41959424 | tf_op jit(solution)/shard_map/while/body/eval_jaxpr/convert_element_type | solution.py:50
  470.9 4.0 fusion.108
  474.9 4.3 fusion.109
  479.2 7.7 %fusion.112 = bf16[2,4096,128]{2,1,0:T(8,128)(2,1)} fusion(bf16[2,4096,128]{2,1,0:T(8,128)(2,1)} %get-tuple-element.204, s32[]{:T(128)} %get-tuple-element.201, bf16[2,1024,128]{1,2,0:T(8,128)(2,1)} %get-tuple-element.217, f32[1024,4096]{1,0:T(8,128)S(1)} %get-tuple-element.187, f32[1024]{0:T(1024)S(1)} %fusion.109, ...), kind=kOutput, calls=%fused_computation.11.clone.1 | convolution fusion | flops 1094713344 | bytes 19149824 | tf_op jit(solution)/shard_map/while/body/eval_jaxpr/qk,qd->kd/dot_general | solution.py:54
  486.9 9.9 %multiply_reduce_fusion.2 = (f32[1024]{0:T(1024)S(1)}, f32[1024,4096]{1,0:T(8,128)}) fusion(f32[1024]{0:T(1024)S(1)} %fusion.109, f32[1024]{0:T(1024)S(1)} %get-tuple-element.188, f32[1024,4096]{1,0:T(8,128)S(1)} %get-tuple-element.187, pred[4096]{0:T(1024)(128)(4,1)S(1)} %compare_reduce_fusion.2, bf16[2,4096,128]{1,2,0:T(8,128)(2,1)S(1)} %copy-done.16, ...), kind=kOutput, calls=%fused_computation.2.clone.1 | convolution fusion | flops 1098906624 | bytes 34882560 | tf_op jit(solution)/shard_map/while/body/eval_jaxpr/qd,kd->qk/dot_general | solution.py:46
  496.8 10.2 %multiply_convert_fusion.4 = bf16[1024,4096]{1,0:T(8,128)(2,1)S(1)} fusion(f32[1024,4096]{1,0:T(8,128)} %get-tuple-element.189, f32[1024]{0:T(1024)S(1)} %get-tuple-element.190, f32[1024]{0:T(1024)S(1)} %fusion.109, f32[1024]{0:T(1024)S(1)} %get-tuple-element.188, f32[1024,4096]{1,0:T(8,128)S(1)} %get-tuple-element.187, ...), kind=kLoop, calls=%fused_computation.1.clone.1 | loop fusion | flops 33554432 | bytes 41959424 | tf_op jit(solution)/shard_map/while/body/eval_jaxpr/convert_element_type | solution.py:50
  507.0 3.5 fusion.111
  521.1 23.2 %reduce-scatter.3.cloned.1.call-done = bf16[1024,256]{1,0:T(8,128)(2,1)} async-done(((bf16[4096,256]{1,0:T(8,128)(2,1)}), bf16[1024,256]{1,0:T(8,128)(2,1)}) %reduce-scatter.3.cloned.1.call-update) | async-done | bytes 524304 | tf_op jit(solution)/shard_map/reduce_scatter | solution.py:191
  544.3 32.5 %reduce-scatter.5.cloned.1.call-done = bf16[1024,256]{1,0:T(8,128)(2,1)} async-done(((bf16[4096,256]{1,0:T(8,128)(2,1)}), bf16[1024,256]{1,0:T(8,128)(2,1)}) %reduce-scatter.5.cloned.1.call-update) | async-done | bytes 524304 | tf_op jit(solution)/shard_map/reduce_scatter | solution.py:194
  (99 shorter events, 46.0 us)
Async XLA Ops:
  19.3 9.8 %copy-start.2 = (bf16[128,4096]{1,0:T(8,128)(2,1)S(1)}, bf16[128,4096]{1,0:T(8,128)(2,1)}, u32[]{:S(2)}) copy-start(bf16[128,4096]{1,0:T(8,128)(2,1)} %param.17) | copy-start | bytes 3145732
  19.3 43.4 %all-to-all-start.1 = ((bf16[32,1,36,1024]{3,2,1,0:T(8,128)(2,1)}), bf16[32,1,36,1024]{3,2,1,0:T(8,128)(2,1)}, u32[]{:S(2)}, u32[]{:S(2)}) async-start(bf16[32,1,36,1024]{3,2,1,0:T(8,128)(2,1)} %bitcast.13), calls=%async_computation.1 | async-start | bytes 5242880 | tf_op jit(solution)/shard_map/all_to_all | solution.py:138
  33.2 6.1 %copy-start.14 = (f32[128,2]{0,1:T(2,128)S(1)}, f32[128,2]{0,1:T(2,128)}, u32[]{:S(2)}) copy-start(f32[128,2]{0,1:T(2,128)} %param.20) | copy-start | bytes 3076
  69.8 133.5 %all-to-all-start = ((bf16[32,1,36,4096]{3,2,1,0:T(8,128)(2,1)}), bf16[32,1,36,4096]{3,2,1,0:T(8,128)(2,1)}, u32[]{:S(2)}, u32[]{:S(2)}) async-start(bf16[32,1,36,4096]{3,2,1,0:T(8,128)(2,1)} %bitcast.200), calls=%async_computation | async-start | bytes 20971520 | tf_op jit(solution)/shard_map/all_to_all | solution.py:131
  203.2 11.2 %copy-start.4 = (bf16[4,8,1,36,1,512]{5,4,3,1,0,2:T(2,128)(2,1)S(1)}, bf16[4,8,1,36,1,512]{5,4,3,1,0,2:T(2,128)(2,1)}, u32[]{:S(2)}) copy-start(bf16[4,8,1,36,1,512]{5,4,3,1,0,2:T(2,128)(2,1)} %get-tuple-element.126) | copy-start | bytes 3538948
  203.3 11.2 %copy-start.5 = (bf16[4,8,1,36,1,512]{5,4,3,1,0,2:T(2,128)(2,1)S(1)}, bf16[4,8,1,36,1,512]{5,4,3,1,0,2:T(2,128)(2,1)}, u32[]{:S(2)}) copy-start(bf16[4,8,1,36,1,512]{5,4,3,1,0,2:T(2,128)(2,1)} %get-tuple-element.127) | copy-start | bytes 3538948
  203.3 11.2 %copy-start.15 = (bf16[1,4096,512]{2,1,0:T(8,128)(2,1)S(1)}, bf16[1,4096,512]{2,1,0:T(8,128)(2,1)}, u32[]{:S(2)}) copy-start(bf16[1,4096,512]{2,1,0:T(8,128)(2,1)} %param.21) | copy-start | bytes 12582916
  213.0 1.5 copy-start.17
  240.1 11.9 %copy-start.7 = (bf16[1024,256]{1,0:T(8,128)(2,1)S(1)}, bf16[1024,256]{1,0:T(8,128)(2,1)}, u32[]{:S(2)}) copy-start(bf16[1024,256]{1,0:T(8,128)(2,1)} %param.14) | copy-start | bytes 1572868
  240.1 13.0 %copy-start.8 = (bf16[1024,256]{1,0:T(8,128)(2,1)S(1)}, bf16[1024,256]{1,0:T(8,128)(2,1)}, u32[]{:S(2)}) copy-start(bf16[1024,256]{1,0:T(8,128)(2,1)} %param.15) | copy-start | bytes 1572868
  240.1 148.0 %all-to-all-start.2 = ((bf16[32,1,36,4096]{3,2,1,0:T(8,128)(2,1)}), bf16[32,1,36,4096]{3,2,1,0:T(8,128)(2,1)}, u32[]{:S(2)}, u32[]{:S(2)}) async-start(bf16[32,1,36,4096]{3,2,1,0:T(8,128)(2,1)} %bitcast.203), calls=%async_computation.2 | async-start | bytes 20971520 | tf_op jit(solution)/shard_map/all_to_all | solution.py:150
  251.9 2.4 copy-start.1
  252.0 2.7 copy-start.13
  252.0 175.7 %all-gather.3.cloned.1.call-start = ((), (), s32[]{:S(2)}) async-start(), calls=%async_computation.6 | async-start | bytes 2621440 | tf_op jit(solution)/shard_map/all_gather | solution.py:181
  253.1 174.6 %all-gather.5.cloned.1.call-start = ((), (), s32[]{:S(2)}) async-start(), calls=%async_computation.7 | async-start | bytes 2621440 | tf_op jit(solution)/shard_map/all_gather | solution.py:182
  408.4 1.2 copy-start.3
  410.4 1.0 copy-start.6
  411.3 5.5 copy-start.9
  412.4 13.9 %all-to-all-start.3 = ((bf16[128,8,256]{0,2,1:T(8,128)(2,1)}), bf16[128,8,256]{0,2,1:T(8,128)(2,1)S(1)}, u32[]{:S(2)}, u32[]{:S(2)}) async-start(bf16[128,8,256]{0,2,1:T(8,128)(2,1)} %bitcast.37), calls=%async_computation.3 | async-start | bytes 1048576 | tf_op jit(solution)/shard_map/all_to_all | solution.py:173
  416.8 127.5 %reduce-scatter.3.cloned.1.call-start = ((), (), s32[]{:S(2)}) async-start(), calls=%async_computation.8 | async-start | bytes 2621440 | tf_op jit(solution)/shard_map/reduce_scatter | solution.py:191
  436.2 7.7 %copy-start.16 = (bf16[2,4096,128]{1,2,0:T(8,128)(2,1)S(1)}, bf16[2,4096,128]{1,2,0:T(8,128)(2,1)}, u32[]{:S(2)}) copy-start(bf16[2,4096,128]{1,2,0:T(8,128)(2,1)} %get-tuple-element.218) | copy-start | bytes 6291460 | tf_op jit(solution)/shard_map/while
  464.0 3.5 copy-start
  464.1 3.5 copy-start.10
  470.0 0.8 copy-start.11
  479.2 7.7 %copy-start.16 = (bf16[2,4096,128]{1,2,0:T(8,128)(2,1)S(1)}, bf16[2,4096,128]{1,2,0:T(8,128)(2,1)}, u32[]{:S(2)}) copy-start(bf16[2,4096,128]{1,2,0:T(8,128)(2,1)} %get-tuple-element.218) | copy-start | bytes 6291460 | tf_op jit(solution)/shard_map/while
  507.0 3.5 copy-start
  507.0 3.5 copy-start.10
  513.0 0.8 copy-start.11
  517.0 59.8 %reduce-scatter.5.cloned.1.call-start = ((), (), s32[]{:S(2)}) async-start(), calls=%async_computation.9 | async-start | bytes 2621440 | tf_op jit(solution)/shard_map/reduce_scatter | solution.py:194
  517.0 3.2 copy-start.12
Sparse Core Ops, SparseCore 0:
  255.0 127.8 all-gather.2
  384.6 32.6 all-gather.4
  517.1 27.1 reduce-scatter.2
  547.3 29.4 reduce-scatter.4
where the time goes:
time: 592 us; the launch traced here: 583 us
  waiting for transfers between devices  331 us (56%)
  matrix products  96.4 us (16%)
  local copies, waits for them, and re-layouts  70.8 us (12%)
  other arithmetic  37.1 us (6%)
  starting transfers between devices  33.8 us (6%)
  between operations  14.2 us (2%)
    all_to_all x1, waiting for transfers between devices, on_device(): lax.all_to_all(term_low.reshape(frame_count * expert_count, local_experts...  133 us
    all_to_all x1, waiting for transfers between devices, on_device(): lax.all_to_all(row_copies.reshape(frame_count * expert_count, local_exper...  115 us
    reduce_scatter x1, waiting for transfers between devices, on_device(): lax.psum_scatter(value_part.astype(jnp.bfloat16), 'frame', scatter_dimens...  32.5 us
    reduce_scatter x1, waiting for transfers between devices, on_device(): lax.psum_scatter(key_part.astype(jnp.bfloat16), 'frame', scatter_dimensio...  23.2 us
    convert_element_type x2, other arithmetic, head_backward(): (softmax * (softmax_grad - centre) * score_scale).astype(jnp.bfloat16)  20.4 us
    dot_general x2, matrix products, head_backward(): jnp.einsum('qd,kd->qk', grad_rows, value_rows, preferred_element_type=jnp...  19.9 us
    all_to_all x1, waiting for transfers between devices, on_device(): lax.all_to_all(send_stored.reshape(frame_count * expert_count, local_expe...  17.9 us
    dot_general x2, matrix products, head_backward(): jnp.einsum('qk,qd->kd', softmax_low, grad_rows, preferred_element_type=jn...  15.4 us
  transfers between devices with their start and end apart: 8, of which 6 were waited for; matrix products, arithmetic and copies ran while one was open for 10% of the time, Pallas kernels for 0%

commit v1 on v0

v1 whole, which is shorter than its diff:
```python
import functools

import jax
import jax.numpy as jnp
from jax import lax
from jax.experimental import pallas as pl
from jax.experimental.pallas import tpu as pltpu
from jax.sharding import PartitionSpec as P

HD = 128
N_EXP = 8
N_FRAME = 4
MAIN = 16
BF = jnp.bfloat16
F32 = jnp.float32
MESH = pl.DeviceIdType.MESH
VMEM_LIMIT = 63 * 1024 * 1024


def dot_nn(a, b):
    return lax.dot_general(a, b, (((1,), (0,)), ((), ())), preferred_element_type=F32)


def dot_nt(a, b):
    return lax.dot_general(a, b, (((1,), (1,)), ((), ())), preferred_element_type=F32)


def moe_kernel(
    ids_ref, gw_ref, og_ref, st_ref, hs_ref, wd_hbm, wg_hbm, wu_hbm,
    resid_ref, gout_ref,
    wd, wg, wu, rows, stored, hid, grads, ysend, yrecv, zrecv,
    half_in, full_in, moe, amat, emat, atmat, etmat,
    w_sem, ys_sem, yr_sem, zs_sem, zr_sem, ag_s, ag_r, fw_s, fw_r, st_s, st_r,
    ha_s, ha_r, fu_s, fu_r, go_s, go_r,
):
    me = lax.axis_index("expert")
    fr = lax.axis_index("frame")
    left = lax.rem(fr + 3, 4)
    right = lax.rem(fr + 1, 4)
    opposite = lax.rem(fr + 2, 4)
    toks, width = og_ref.shape
    cw = width // 4
    ext = cw // 4
    ff = hid.shape[2]
    n_rows = rows.shape[2]
    half = n_rows // 2

    def to_frame(src, dst, ss, rs, dest):
        return pltpu.make_async_remote_copy(
            src_ref=src, dst_ref=dst, send_sem=ss, recv_sem=rs,
            device_id={"frame": dest}, device_id_type=MESH)

    def to_expert(src, dst, ss, rs, dest):
        return pltpu.make_async_remote_copy(
            src_ref=src, dst_ref=dst, send_sem=ss, recv_sem=rs,
            device_id={"expert": dest}, device_id_type=MESH)

    barrier = pltpu.get_barrier_semaphore()
    for d in range(1, N_EXP):
        pl.semaphore_signal(barrier, inc=1, device_id={"expert": lax.rem(me + d, N_EXP)}, device_id_type=MESH)
    for dest in (left, right, opposite):
        pl.semaphore_signal(barrier, inc=1, device_id={"frame": dest}, device_id_type=MESH)

    w_copies = [pltpu.make_async_copy(wd_hbm.at[:, pl.ds(c * cw, cw)], wd.at[c], w_sem.at[c]) for c in range(4)]
    w_copies += [pltpu.make_async_copy(wg_hbm, wg, w_sem.at[4]), pltpu.make_async_copy(wu_hbm, wu, w_sem.at[5])]
    for copy in w_copies:
        copy.start()

    earlier_mask = (
        lax.broadcasted_iota(jnp.int32, (toks, toks), 0) < lax.broadcasted_iota(jnp.int32, (toks, toks), 1)
    ).astype(F32).astype(BF)
    expert_iota = lax.broadcasted_iota(jnp.int32, (N_EXP, toks), 0)
    base = jnp.zeros((N_EXP, 1), F32)
    main_iota = lax.broadcasted_iota(jnp.int32, (2 * N_EXP * MAIN, toks), 0)
    ext_iota = lax.broadcasted_iota(jnp.int32, (N_EXP * MAIN, toks), 0)
    main_sum = jnp.zeros(main_iota.shape, F32)
    ext_sum = [jnp.zeros(ext_iota.shape, F32) for _ in range(4)]
    for k in range(2):
        rel = (ids_ref[pl.ds(k, 1), :] - me + N_EXP) & (N_EXP - 1)
        hit = (expert_iota == rel).astype(F32)
        earlier = dot_nn(hit.astype(BF), earlier_mask) + base
        slot = jnp.sum(hit * earlier, axis=0, keepdims=True).astype(jnp.int32)
        base = base + jnp.sum(hit, axis=1, keepdims=True)
        main_at = jnp.where(slot < 32, (slot >> 4) * (N_EXP * MAIN) + rel * MAIN + (slot & 15), -1)
        ext_at = jnp.where(slot < 32, -1000, rel * MAIN + slot - 32)
        main_k = (main_iota == main_at).astype(F32)
        amat[:, pl.ds(k * toks, toks)] = main_k.astype(BF)
        main_sum = main_sum + main_k
        for j in range(4):
            ext_k = (ext_iota == ext_at + 4 * j).astype(F32)
            emat[j, :, pl.ds(k * toks, toks)] = ext_k.astype(BF)
            ext_sum[j] = ext_sum[j] + ext_k
    atmat[...] = main_sum.T.astype(BF)
    for j in range(4):
        etmat[j] = ext_sum[j].T.astype(BF)

    def pack_pairs(chunk, pairs):
        main = dot_nn(amat[...], pairs).astype(BF)
        ysend[chunk, :, pl.ds(0, cw)] = main[: N_EXP * MAIN]
        ysend[chunk, :, pl.ds(cw, cw)] = main[N_EXP * MAIN:]
        extra = dot_nn(emat[0], pairs[:, :ext])
        for j in range(1, 4):
            extra = extra + dot_nn(emat[j], pairs[:, j * ext:(j + 1) * ext])
        ysend[chunk, :, pl.ds(2 * cw, ext)] = extra.astype(BF)

    def y_copy(chunk, d):
        return to_expert(
            ysend.at[chunk, pl.ds(MAIN * d, MAIN)], yrecv.at[chunk, pl.ds(MAIN * d, MAIN)],
            ys_sem.at[chunk, d], yr_sem.at[chunk, d], lax.rem(me + d, N_EXP))

    pl.semaphore_wait(barrier, N_EXP + 2)

    def build_rows(c, carry):
        x = og_ref[:, pl.ds(pl.multiple_of(c * cw, cw), cw)].astype(F32)
        pairs = jnp.concatenate(
            [(gw_ref[:, 0:1] * x).astype(BF), (gw_ref[:, 1:2] * x).astype(BF)], axis=0)
        pack_pairs(c, pairs)
        for d in range(1, N_EXP):
            y_copy(c, d).start()
        return carry

    lax.fori_loop(0, 4, build_rows, 0)

    def build_stored(c, carry):
        f = lax.rem(fr + c, 4)
        parts = []
        for k in range(2):
            parts.append(jnp.concatenate(
                [st_ref[:, pl.ds(pl.multiple_of((k * 2 + kind) * 4 * ff + f * ff, ff), ff)] for kind in range(2)], axis=1))
        pack_pairs(4 + c, jnp.concatenate(parts, axis=0))
        for d in range(1, N_EXP):
            y_copy(4 + c, d).start()
        return carry

    lax.fori_loop(0, 4, build_stored, 0)

    sel_r = lax.broadcasted_iota(jnp.int32, (4 * N_EXP, N_EXP * MAIN), 0)
    sel_c = lax.broadcasted_iota(jnp.int32, (4 * N_EXP, N_EXP * MAIN), 1)
    selt_r = lax.broadcasted_iota(jnp.int32, (N_EXP * MAIN, 4 * N_EXP), 1)
    selt_c = lax.broadcasted_iota(jnp.int32, (N_EXP * MAIN, 4 * N_EXP), 0)

    def unpack(chunk, dst):
        for d in range(1, N_EXP):
            y_copy(chunk, d).wait_recv()
        yrecv[chunk, pl.ds(0, MAIN)] = ysend[chunk, pl.ds(0, MAIN)]
        dst[pl.ds(0, N_EXP * MAIN), :] = yrecv[chunk, :, pl.ds(0, cw)]
        dst[pl.ds(N_EXP * MAIN, N_EXP * MAIN), :] = yrecv[chunk, :, pl.ds(cw, cw)]
        extra = yrecv[chunk, :, pl.ds(2 * cw, ext)]
        for j in range(4):
            sel = (sel_c == (sel_r >> 2) * MAIN + 4 * j + (sel_r & 3)).astype(F32).astype(BF)
            dst[pl.ds(2 * N_EXP * MAIN, 4 * N_EXP), pl.ds(j * ext, ext)] = dot_nn(sel, extra).astype(BF)

    def ag_copy(c, side):
        return to_frame(rows.at[0, c], rows.at[1 + side, c], ag_s.at[c, side], ag_r.at[c, side],
                        right if side == 0 else left)

    def fw_copy(c, side):
        part = pl.ds(side * half, half)
        return to_frame(rows.at[1 + side, c, part], rows.at[3, c, part], fw_s.at[c, side], fw_r.at[c, side],
                        right if side == 0 else left)

    def add_hidden(b, c):
        hid[b] += dot_nt(rows[b, c], wd[c])

    hid[...] = jnp.zeros_like(hid)
    for copy in w_copies[:4]:
        copy.wait()

    def own_rows(c, carry):
        unpack(c, rows.at[0, c])
        ag_copy(c, 0).start()
        ag_copy(c, 1).start()
        add_hidden(0, c)
        return carry

    lax.fori_loop(0, 4, own_rows, 0)

    def next_rows(c, carry):
        for side in range(2):
            ag_copy(c, side).wait_recv()
            fw_copy(c, side).start()
        add_hidden(1, c)
        add_hidden(2, c)
        return carry

    lax.fori_loop(0, 4, next_rows, 0)

    def own_stored(c, carry):
        unpack(4 + c, sbuf_at(c))
        return carry

    def sbuf_at(c):
        return grads.at[c]

    lax.fori_loop(0, 4, own_stored, 0)
    st_copies = [
        to_frame(grads.at[1], stored.at[0], st_s.at[0], st_r.at[0], right),
        to_frame(grads.at[3], stored.at[1], st_s.at[1], st_r.at[1], left),
        to_frame(grads.at[2], stored.at[2], st_s.at[2], st_r.at[2], opposite),
    ]
    for i in (2, 0, 1):
        st_copies[i].start()

    def far_rows(c, carry):
        for side in range(2):
            fw_copy(c, side).wait_recv()
        add_hidden(3, c)
        return carry

    lax.fori_loop(0, 4, far_rows, 0)

    def hidden_to_grads(b, src):
        h = hid[b]
        g = src[:, pl.ds(0, ff)].astype(F32)
        u = src[:, pl.ds(ff, ff)].astype(F32)
        s = 1.0 / (1.0 + jnp.exp(-g))
        gate = (h * u * s * (1.0 + g * (1.0 - s))).astype(BF)
        up = (h * g * s).astype(BF)
        return gate, up

    for i in (2, 0, 1):
        st_copies[i].wait()
    for b in (3, 2, 1, 0):
        src = grads.at[0] if b == 0 else stored.at[b - 1]
        gate, up = hidden_to_grads(b, src)
        grads[b, :, pl.ds(0, ff)] = gate
        grads[b, :, pl.ds(ff, ff)] = up

    for copy in w_copies[4:]:
        copy.wait()

    def term(b, c):
        at = pl.ds(pl.multiple_of(c * cw, cw), cw)
        return dot_nt(grads[b, :, pl.ds(0, ff)], wg[at, :]) + dot_nt(grads[b, :, pl.ds(ff, ff)], wu[at, :])

    def ha_copy(c, side):
        return to_frame(rows.at[3, c, pl.ds(side * half, half)], half_in.at[side, c],
                        ha_s.at[c, side], ha_r.at[c, side], right if side == 0 else left)

    def fu_copy(c, side):
        return to_frame(rows.at[2 - side, c], full_in.at[side, c], fu_s.at[c, side], fu_r.at[c, side],
                        right if side == 0 else left)

    def far_terms(c, carry):
        rows[3, c] = term(3, c).astype(BF)
        for side in range(2):
            ha_copy(c, side).start()
        return carry

    lax.fori_loop(0, 4, far_terms, 0)

    def near_terms(c, carry):
        for side in range(2):
            fw_copy(c, 1 - side).wait_send()
            part = term(2 - side, c)
            ha_copy(c, side).wait_recv()
            lo = side * half
            rows[2 - side, c, pl.ds(half - lo, half)] = part[half - lo:half - lo + half].astype(BF)
            rows[2 - side, c, pl.ds(lo, half)] = (
                part[lo:lo + half].astype(BF).astype(F32) + half_in[side, c].astype(F32)).astype(BF)
            fu_copy(c, side).start()
        return carry

    lax.fori_loop(0, 4, near_terms, 0)

    def z_copy(c, d):
        return to_expert(
            ysend.at[c, pl.ds(MAIN * d, MAIN)], zrecv.at[c, pl.ds(MAIN * d, MAIN)],
            zs_sem.at[c, d], zr_sem.at[c, d], lax.rem(me + N_EXP - d, N_EXP))

    def own_terms(c, carry):
        part = term(0, c).astype(BF).astype(F32)
        for side in range(2):
            fu_copy(c, side).wait_recv()
        total = (part + full_in[0, c].astype(F32) + full_in[1, c].astype(F32)).astype(BF)
        for d in range(1, N_EXP):
            y_copy(c, d).wait_send()
        ysend[c, :, pl.ds(0, cw)] = total[: N_EXP * MAIN]
        ysend[c, :, pl.ds(cw, cw)] = total[N_EXP * MAIN: 2 * N_EXP * MAIN]
        extra = jnp.zeros((N_EXP * MAIN, ext), F32)
        for j in range(4):
            sel = (selt_c == (selt_r >> 2) * MAIN + 4 * j + (selt_r & 3)).astype(F32).astype(BF)
            extra = extra + dot_nn(sel, total[2 * N_EXP * MAIN:, j * ext:(j + 1) * ext])
        ysend[c, :, pl.ds(2 * cw, ext)] = extra.astype(BF)
        for d in range(1, N_EXP):
            z_copy(c, d).start()
        return carry

    lax.fori_loop(0, 4, own_terms, 0)

    def square_sum(c, acc):
        x = hs_ref[:, pl.ds(pl.multiple_of(c * cw, cw), cw)].astype(F32)
        return acc + jnp.sum(x * x, axis=1, keepdims=True)

    inv = lax.rsqrt(lax.fori_loop(0, 4, square_sum, jnp.zeros((toks, 1), F32)) / width + 1e-6)

    def combine(c, acc):
        for d in range(1, N_EXP):
            z_copy(c, d).wait_recv()
        zrecv[c, pl.ds(0, MAIN)] = ysend[c, pl.ds(0, MAIN)]
        at = pl.ds(pl.multiple_of(c * cw, cw), cw)
        got = dot_nn(atmat[:, pl.ds(0, N_EXP * MAIN)], zrecv[c, :, pl.ds(0, cw)])
        got = got + dot_nn(atmat[:, pl.ds(N_EXP * MAIN, N_EXP * MAIN)], zrecv[c, :, pl.ds(cw, cw)])
        extra = zrecv[c, :, pl.ds(2 * cw, ext)]
        got = got + jnp.concatenate([dot_nn(etmat[j], extra) for j in range(4)], axis=1)
        moe[:, at] = got
        return acc + jnp.sum(got * hs_ref[:, at].astype(F32), axis=1, keepdims=True)

    mean = lax.fori_loop(0, 4, combine, jnp.zeros((toks, 1), F32)) * inv / width

    def residual(c, carry):
        at = pl.ds(pl.multiple_of(c * cw, cw), cw)
        n = hs_ref[:, at].astype(F32) * inv
        resid_ref[:, at] = (og_ref[:, at].astype(F32) + inv * (moe[:, at] - n * mean)).astype(BF)
        return carry

    lax.fori_loop(0, 4, residual, 0)

    hw = gout_ref.shape[1]
    own_at = pl.ds(pl.multiple_of(me * toks, toks), toks)

    def go_copy(d):
        dest = lax.rem(me + d, N_EXP)
        return to_expert(
            resid_ref.at[:, pl.ds(pl.multiple_of(dest * hw, hw), hw)], gout_ref.at[own_at],
            go_s.at[d], go_r.at[d], dest)

    for d in range(1, N_EXP):
        go_copy(d).start()
    gout_ref[own_at, :] = resid_ref[:, pl.ds(pl.multiple_of(me * hw, hw), hw)]

    def drain(c, carry):
        for side in range(2):
            ag_copy(c, side).wait_send()
            ha_copy(c, side).wait_send()
            fu_copy(c, side).wait_send()
        for d in range(1, N_EXP):
            y_copy(4 + c, d).wait_send()
            z_copy(c, d).wait_send()
        return carry

    lax.fori_loop(0, 4, drain, 0)
    for d in range(1, N_EXP):
        go_copy(d).wait()


def moe_call(ids_t, gate_weights, out_grad, stored, hidden_state, wd, wg, wu, att_local):
    toks, width = out_grad.shape
    ff = wd.shape[0]
    cw = width // 4
    n_rows = N_EXP * 36
    pw = 2 * cw + cw // 4
    vm = pl.BlockSpec(memory_space=pltpu.VMEM)
    hbm = pl.BlockSpec(memory_space=pl.ANY)
    dma = pltpu.SemaphoreType.DMA
    return pl.pallas_call(
        moe_kernel,
        out_shape=(
            jax.ShapeDtypeStruct((toks, width), BF),
            jax.ShapeDtypeStruct((toks * N_EXP, att_local), BF),
        ),
        in_specs=[vm] * 5 + [hbm] * 3,
        out_specs=(vm, vm),
        scratch_shapes=[
            pltpu.VMEM((4, ff, cw), BF),
            pltpu.VMEM((width, ff), BF),
            pltpu.VMEM((width, ff), BF),
            pltpu.VMEM((4, 4, n_rows, cw), BF),
            pltpu.VMEM((3, n_rows, 2 * ff), BF),
            pltpu.VMEM((4, n_rows, ff), F32),
            pltpu.VMEM((4, n_rows, 2 * ff), BF),
            pltpu.VMEM((8, N_EXP * MAIN, pw), BF),
            pltpu.VMEM((8, N_EXP * MAIN, pw), BF),
            pltpu.VMEM((4, N_EXP * MAIN, pw), BF),
            pltpu.VMEM((2, 4, n_rows // 2, cw), BF),
            pltpu.VMEM((2, 4, n_rows, cw), BF),
            pltpu.VMEM((toks, width), F32),
            pltpu.VMEM((2 * N_EXP * MAIN, 2 * toks), BF),
            pltpu.VMEM((4, N_EXP * MAIN, 2 * toks), BF),
            pltpu.VMEM((toks, 2 * N_EXP * MAIN), BF),
            pltpu.VMEM((4, toks, N_EXP * MAIN), BF),
            dma((6,)), dma((8, 8)), dma((8, 8)), dma((4, 8)), dma((4, 8)),
            dma((4, 2)), dma((4, 2)), dma((4, 2)), dma((4, 2)), dma((3,)), dma((3,)),
            dma((4, 2)), dma((4, 2)), dma((4, 2)), dma((4, 2)), dma((8,)), dma((8,)),
        ],
        compiler_params=pltpu.CompilerParams(
            collective_id=0, has_side_effects=True, vmem_limit_bytes=VMEM_LIMIT),
        cost_estimate=pl.CostEstimate(flops=15 * 10**9, bytes_accessed=20 * 10**6, transcendentals=0),
        name="moe",
    )(ids_t, gate_weights, out_grad, stored, hidden_state, wd, wg, wu)


def attention_kernel(q_ref, k_ref, v_ref, go_ref, dq_ref, dk_ref, dv_ref, probs):
    fr = lax.axis_index("frame")
    span = q_ref.shape[0]
    qt_w = 512
    scale = HD ** -0.5
    log2e = 1.4426950408889634
    dk_ref[...] = jnp.zeros_like(dk_ref)
    dv_ref[...] = jnp.zeros_like(dv_ref)
    for h in range(2):
        cols = pl.ds(h * HD, HD)
        for qi in range(span // qt_w):
            qrows = pl.ds(qi * qt_w, qt_w)
            q = q_ref[qrows, cols]
            qt = q.astype(F32).T.astype(BF)

            def krows(s):
                return pl.ds(pl.multiple_of(s * span, span), span)

            def largest(s, m):
                sc = dot_nn(k_ref[krows(s), cols], qt) * (scale * log2e)
                return jnp.maximum(m, jnp.max(sc, axis=0, keepdims=True))

            m = lax.fori_loop(0, fr + 1, largest, jnp.full((1, qt_w), -1e30, F32))

            def forward(s, carry):
                l, o = carry
                sc = dot_nn(k_ref[krows(s), cols], qt) * (scale * log2e)
                p = jnp.exp2(sc - m)
                low = p.astype(BF)
                probs[s] = low
                vt = v_ref[krows(s), cols].astype(F32).T.astype(BF)
                return l + jnp.sum(p, axis=0, keepdims=True), o + dot_nn(vt, low)

            l, o = lax.fori_loop(
                0, fr + 1, forward, (jnp.zeros((1, qt_w), F32), jnp.zeros((HD, qt_w), F32)))
            inv = 1.0 / l
            got = go_ref[qrows, cols].astype(F32).T * inv
            go_n = got.astype(BF)
            go_s = (got * scale).astype(BF)
            centre = jnp.sum(go_s.astype(F32) * (o * inv), axis=0, keepdims=True)
            go_rows = go_n.astype(F32).T.astype(BF)

            def backward(s, dq):
                kk = k_ref[krows(s), cols]
                p = probs[s]
                dp = dot_nn(v_ref[krows(s), cols], go_s)
                ds = (p.astype(F32) * (dp - centre)).astype(BF)
                dk_ref[krows(s), cols] += dot_nn(ds, q)
                dv_ref[krows(s), cols] += dot_nn(p, go_rows)
                kt = kk.astype(F32).T.astype(BF)
                return dq + dot_nn(kt, ds)

            dq = lax.fori_loop(0, fr + 1, backward, jnp.zeros((HD, qt_w), F32))
            dq_ref[qrows, cols] = dq.T.astype(BF)


def attention_call(q, k, v, go):
    span, width = q.shape
    vm = pl.BlockSpec(memory_space=pltpu.VMEM)
    return pl.pallas_call(
        attention_kernel,
        out_shape=(
            jax.ShapeDtypeStruct(q.shape, BF),
            jax.ShapeDtypeStruct(k.shape, F32),
            jax.ShapeDtypeStruct(v.shape, F32),
        ),
        in_specs=[vm] * 4,
        out_specs=(vm,) * 3,
        scratch_shapes=[pltpu.VMEM((4, span, 512), BF)],
        compiler_params=pltpu.CompilerParams(vmem_limit_bytes=VMEM_LIMIT),
        cost_estimate=pl.CostEstimate(flops=10 * 10**9, bytes_accessed=20 * 10**6, transcendentals=0),
        name="attention",
    )(q, k, v, go)


def on_device(
    queries, keys, values, hidden_state, out_grad, stored_pre, expert_ids, gate_weights,
    w_gate, w_up, w_down,
):
    toks = out_grad.shape[0]
    key_all, value_all = (
        lax.all_gather(keys, "frame", axis=0, tiled=True),
        lax.all_gather(values, "frame", axis=0, tiled=True),
    )
    resid, go = moe_call(
        expert_ids.T, gate_weights, out_grad, stored_pre.reshape(toks, -1), hidden_state,
        w_down[0], w_gate[0], w_up[0], queries.shape[1])
    dq, dk, dv = attention_call(queries, key_all, value_all, go)
    dk = lax.psum_scatter(dk.astype(BF), "frame", scatter_dimension=0, tiled=True)
    dv = lax.psum_scatter(dv.astype(BF), "frame", scatter_dimension=0, tiled=True)
    return resid, dq, dk, dv


def solution(mesh):
    rows = P(("dp", "frame"), "expert")
    toks = ("dp", "frame", "expert")
    return jax.shard_map(
        on_device,
        mesh=mesh,
        in_specs=(
            rows, rows, rows, P(toks, None), P(toks, None), P(toks, None, None, None),
            P(toks, None), P(toks, None), P("expert", None, "frame"), P("expert", None, "frame"),
            P("expert", "frame", None),
        ),
        out_specs=(P(toks, None), rows, rows, rows),
        check_vma=False,
    )
```

time: 592 us -> 380 us (0.64); the launches traced: 583 us -> 380 us
  Pallas kernels: 0 us -> 266 us
  waiting for transfers between devices: 331 us -> 86 us
  matrix products: 96.4 us -> 0 us
  local copies, waits for them, and re-layouts: 70.8 us -> 6.85 us
  starting transfers between devices: 33.8 us -> 0.16 us
  other arithmetic: 37.1 us -> 7.46 us
    all_to_all x4 -> x0, waiting for transfers between devices: 275 us -> none  [the longest x1 133 us: on_device(): lax.all_to_all(term_low.reshape(frame_count * expert_count, local_experts...]
    pallas_call x0 -> x2, Pallas kernels: none -> 266 us  [the longest x1 249 us: moe_call(): pl.pallas_call(moe_kernel, out_shape=(jax.ShapeDtypeStruct((toks, width),...]
    dot_general x16 -> x0, matrix products: 96.4 us -> none  [the longest x2 19.9 us: head_backward(): jnp.einsum('qd,kd->qk', grad_rows, value_rows, preferred_element_type=jnp...]
    all_to_all x4 -> x0, starting transfers between devices: 33.7 us -> none  [the longest x1 11.8 us: on_device(): lax.all_to_all(term_low.reshape(frame_count * expert_count, local_experts...]
    reduce_scatter x2, waiting for transfers between devices: 55.7 us -> 84.6 us  [the longest x1 52.1 us: on_device(): lax.psum_scatter(dk.astype(BF), 'frame', scatter_dimension=0, tiled=True)]
    reshape x5 -> x1, local copies, waits for them, and re-layouts: 24 us -> 4.46 us  [on_device(): stored_pre.reshape(toks, -1)]
    reduce_sum x6 -> x0, other arithmetic: 15.2 us -> none  [the longest x2 8.65 us: head_backward(): softmax = exponent / jnp.sum(exponent, axis=-1, keepdims=True)]
    convert_element_type x4 -> x2, other arithmetic: 21.1 us -> 7.46 us  [the longest x1 3.75 us: on_device(): dk.astype(BF)]
  transfers between devices with their start and end apart: 8 -> 4, of which waited for: 6 -> 2; matrix products, arithmetic and copies ran while one was open for 10% -> 3% of each run, Pallas kernels for 0% -> 65%
where the time goes in v1:
time: 380 us
  Pallas kernels  266 us (70%)
  waiting for transfers between devices  86 us (23%)
  between operations  13.8 us (4%)
  other arithmetic  7.46 us (2%)
  local copies, waits for them, and re-layouts  6.85 us (2%)
    pallas_call x1, Pallas kernels, moe_call(): pl.pallas_call(moe_kernel, out_shape=(jax.ShapeDtypeStruct((toks, width),...  249 us
    reduce_scatter x1, waiting for transfers between devices, on_device(): lax.psum_scatter(dk.astype(BF), 'frame', scatter_dimension=0, tiled=True)  52.1 us
    reduce_scatter x1, waiting for transfers between devices, on_device(): lax.psum_scatter(dv.astype(BF), 'frame', scatter_dimension=0, tiled=True)  32.4 us
    pallas_call x1, Pallas kernels, attention_call(): pl.pallas_call(attention_kernel, out_shape=(jax.ShapeDtypeStruct(q.shape,...  17.2 us
  transfers between devices with their start and end apart: 4, of which 2 were waited for; matrix products, arithmetic and copies ran while one was open for 3% of the time, Pallas kernels for 65%

profile of v1, /device:TPU:1, one launch (start us, length us, event | category | flops | bytes accessed | tf_op | source)
XLA Modules:
  0.0 380.1 jit_solution(12926809828814727152)
XLA Ops:
  7.2 0.0 all-gather.3.cloned.1.call-start
  7.2 0.7 all-gather.3.cloned.1.call-update
  7.9 0.0 all-gather.5.cloned.1.call-start
  7.9 0.7 all-gather.5.cloned.1.call-update
  8.6 0.0 reduce-scatter.3.cloned.1.call-start
  8.7 1.4 copy.15.gw_ref
  10.1 4.5 %reshape.11.st_ref = bf16[128,8192]{1,0:T(8,128)(2,1)} reshape(bf16[128,2,2,2048]{3,2,1,0:T(2,128)(2,1)} %param.16) | data formatting | bytes 4194304 | tf_op jit(solution)/shard_map/reshape | solution.py:478
  14.6 248.6 %moe.1 = (bf16[128,4096]{1,0:T(8,128)(2,1)}, bf16[1024,256]{1,0:T(8,128)(2,1)}) custom-call(s32[2,128]{1,0:T(2,128)} %bitcast.7, f32[128,2]{1,0:T(8,128)} %copy.15.gw_ref, bf16[128,4096]{1,0:T(8,128)(2,1)} %og_ref.1, bf16[128,8192]{1,0:T(8,128)(2,1)} %reshape.11.st_ref, bf16[128,4096]{1,0:T(8,128)(2,1)} %hs_ref.1, bf16[512,4096]{1,0:T(8,128)(2,1)} %bitcast.4, ...), custom_call_target="tpu_custom_call" | custom-call | flops 15000000512 | bytes 20000000 | tf_op jit(solution)/shard_map/moe/pallas_call | solution.py:356
  263.1 0.0 all-gather.3.cloned.1.call-done.k_ref
  263.2 0.0 all-gather.5.cloned.1.call-done.v_ref
  263.2 17.2 %attention.1 = (bf16[1024,256]{1,0:T(8,128)(2,1)}, f32[4096,256]{1,0:T(8,128)}, f32[4096,256]{1,0:T(8,128)}) custom-call(bf16[1024,256]{1,0:T(8,128)(2,1)} %q_ref.1, bf16[4096,256]{1,0:T(8,128)(2,1)} %all-gather.3.cloned.1.call-done.k_ref, bf16[4096,256]{1,0:T(8,128)(2,1)} %all-gather.5.cloned.1.call-done.v_ref, bf16[1024,256]{1,0:T(8,128)(2,1)} %get-tuple-element.10.go_ref), custom_call_target="tpu_custom_call" | custom-call | flops 10000000000 | bytes 20000000 | tf_op jit(solution)/shard_map/attention/pallas_call | solution.py:452
  280.4 3.8 convert_element_type.6
  284.2 0.0 reduce-scatter.3.cloned.1.call-update
  284.2 0.0 reduce-scatter.5.cloned.1.call-start
  284.3 3.7 convert_element_type.7
  288.0 0.0 copy-start
  288.0 0.0 reduce-scatter.5.cloned.1.call-update
  288.0 52.1 %reduce-scatter.3.cloned.1.call-done = bf16[1024,256]{1,0:T(8,128)(2,1)} async-done(((bf16[4096,256]{1,0:T(8,128)(2,1)}), bf16[1024,256]{1,0:T(8,128)(2,1)}) %reduce-scatter.3.cloned.1.call-update) | async-done | bytes 524304 | tf_op jit(solution)/shard_map/reduce_scatter | solution.py:481
  340.1 32.4 %reduce-scatter.5.cloned.1.call-done = bf16[1024,256]{1,0:T(8,128)(2,1)} async-done(((bf16[4096,256]{1,0:T(8,128)(2,1)}), bf16[1024,256]{1,0:T(8,128)(2,1)}) %reduce-scatter.5.cloned.1.call-update) | async-done | bytes 524304 | tf_op jit(solution)/shard_map/reduce_scatter | solution.py:482
  372.6 0.0 copy-done
  372.6 1.0 copy.17
Async XLA Ops:
  7.2 256.0 %all-gather.3.cloned.1.call-start = ((), (), s32[]{:S(2)}) async-start(), calls=%async_computation.2 | async-start | bytes 2621440 | tf_op jit(solution)/shard_map/all_gather | solution.py:474
  7.9 255.3 %all-gather.5.cloned.1.call-start = ((), (), s32[]{:S(2)}) async-start(), calls=%async_computation.3 | async-start | bytes 2621440 | tf_op jit(solution)/shard_map/all_gather | solution.py:475
  8.6 331.5 %reduce-scatter.3.cloned.1.call-start = ((), (), s32[]{:S(2)}) async-start(), calls=%async_computation.4 | async-start | bytes 2621440 | tf_op jit(solution)/shard_map/reduce_scatter | solution.py:481
  284.2 88.4 %reduce-scatter.5.cloned.1.call-start = ((), (), s32[]{:S(2)}) async-start(), calls=%async_computation.5 | async-start | bytes 2621440 | tf_op jit(solution)/shard_map/reduce_scatter | solution.py:482
  288.0 84.6 %copy-start = (bf16[128,4096]{1,0:T(8,128)(2,1)S(1)}, bf16[128,4096]{1,0:T(8,128)(2,1)}, u32[]{:S(2)}) copy-start(bf16[128,4096]{1,0:T(8,128)(2,1)} %get-tuple-element.18) | copy-start | bytes 3145732
Sparse Core Ops, SparseCore 0:
  9.7 42.7 all-gather.2
  54.1 49.4 all-gather.4
  284.3 55.7 reduce-scatter.2
  343.1 29.4 reduce-scatter.4

commit v2 on v1

--- a/solution.py
+++ b/solution.py
@@ -390,76 +390,192 @@
     )(ids_t, gate_weights, out_grad, stored, hidden_state, wd, wg, wu)
 
 
-def attention_kernel(q_ref, k_ref, v_ref, go_ref, dq_ref, dk_ref, dv_ref, probs):
+def attention_kernel(
+    q_ref, k_ref, v_ref, go_ref, dq_ref, dk_ref, dv_ref,
+    probs, qt, vt, gs_t, g_rows, dqt, send, half_in, full_in,
+    hs, hr, fs, fr_sem,
+):
     fr = lax.axis_index("frame")
+    left = lax.rem(fr + 3, 4)
+    right = lax.rem(fr + 1, 4)
     span = q_ref.shape[0]
-    qt_w = 512
+    tile = 256
+    tiles = span // tile
     scale = HD ** -0.5
     log2e = 1.4426950408889634
-    dk_ref[...] = jnp.zeros_like(dk_ref)
-    dv_ref[...] = jnp.zeros_like(dv_ref)
+
+    barrier = pltpu.get_barrier_semaphore()
+    for dest in (left, right):
+        pl.semaphore_signal(barrier, inc=1, device_id={"frame": dest}, device_id_type=MESH)
+    pl.semaphore_wait(barrier, 2)
+
+    def to_frame(src, dst, ss, rs, dest):
+        return pltpu.make_async_remote_copy(
+            src_ref=src, dst_ref=dst, send_sem=ss, recv_sem=rs,
+            device_id={"frame": dest}, device_id_type=MESH)
+
+    def half_copy(h):
+        return to_frame(send.at[0, h], half_in.at[h], hs.at[h], hr.at[h], left if h == 0 else right)
+
+    def full_copy(side, h):
+        return to_frame(send.at[1 + side, h], full_in.at[side, h], fs.at[side, h], fr_sem.at[side, h],
+                        left if side == 0 else right)
+
+    def rows_at(s, t):
+        return pl.ds(pl.multiple_of(s * span + t * tile, tile), tile)
+
+    def add_half(side, h):
+        half_copy(h).wait_recv()
+        for j in range(2):
+            send[1 + side, h, j] = (send[1 + side, h, j].astype(F32) + half_in[h, j].astype(F32)).astype(BF)
+
     for h in range(2):
         cols = pl.ds(h * HD, HD)
-        for qi in range(span // qt_w):
-            qrows = pl.ds(qi * qt_w, qt_w)
-            q = q_ref[qrows, cols]
-            qt = q.astype(F32).T.astype(BF)
-
-            def krows(s):
-                return pl.ds(pl.multiple_of(s * span, span), span)
-
-            def largest(s, m):
-                sc = dot_nn(k_ref[krows(s), cols], qt) * (scale * log2e)
-                return jnp.maximum(m, jnp.max(sc, axis=0, keepdims=True))
-
-            m = lax.fori_loop(0, fr + 1, largest, jnp.full((1, qt_w), -1e30, F32))
-
-            def forward(s, carry):
-                l, o = carry
-                sc = dot_nn(k_ref[krows(s), cols], qt) * (scale * log2e)
-                p = jnp.exp2(sc - m)
-                low = p.astype(BF)
-                probs[s] = low
-                vt = v_ref[krows(s), cols].astype(F32).T.astype(BF)
-                return l + jnp.sum(p, axis=0, keepdims=True), o + dot_nn(vt, low)
-
-            l, o = lax.fori_loop(
-                0, fr + 1, forward, (jnp.zeros((1, qt_w), F32), jnp.zeros((HD, qt_w), F32)))
-            inv = 1.0 / l
-            got = go_ref[qrows, cols].astype(F32).T * inv
-            go_n = got.astype(BF)
-            go_s = (got * scale).astype(BF)
-            centre = jnp.sum(go_s.astype(F32) * (o * inv), axis=0, keepdims=True)
-            go_rows = go_n.astype(F32).T.astype(BF)
-
-            def backward(s, dq):
-                kk = k_ref[krows(s), cols]
-                p = probs[s]
-                dp = dot_nn(v_ref[krows(s), cols], go_s)
+        qt[...] = q_ref[:, cols].astype(F32).T.astype(BF)
+
+        def largest(i, m):
+            sc = dot_nn(k_ref[rows_at(0, i), cols], qt[...])
+            return jnp.maximum(m, jnp.max(sc, axis=0, keepdims=True))
+
+        n_tiles = (fr + 1) * tiles
+        m = lax.fori_loop(0, n_tiles, largest, jnp.full((1, span), -jnp.inf, F32)) * (scale * log2e)
+
+        def forward(i, carry):
+            l, o = carry
+            sc = dot_nn(k_ref[rows_at(0, i), cols], qt[...])
+            p = jnp.exp2(sc * (scale * log2e) - m)
+            low = p.astype(BF)
+            probs[rows_at(0, i), :] = low
+            v_t = v_ref[rows_at(0, i), cols].astype(F32).T.astype(BF)
+            return l + jnp.sum(p, axis=0, keepdims=True), o + dot_nn(v_t, low)
+
+        l, o = lax.fori_loop(
+            0, n_tiles, forward, (jnp.zeros((1, span), F32), jnp.zeros((HD, span), F32)))
+        inv = 1.0 / l
+        got = go_ref[:, cols].astype(F32).T * inv
+        gs_t[...] = (got * scale).astype(BF)
+        g_rows[...] = got.T.astype(BF)
+        centre = jnp.sum(gs_t[...].astype(F32) * (o * inv), axis=0, keepdims=True)
+        dqt[...] = jnp.zeros_like(dqt)
+
+        def backward(s, slot):
+            def step(t, carry):
+                at = rows_at(s, t)
+                to = rows_at(0, t)
+                kk = k_ref[at, cols]
+                p = probs[at, :]
+                dp = dot_nn(v_ref[at, cols], gs_t[...])
                 ds = (p.astype(F32) * (dp - centre)).astype(BF)
-                dk_ref[krows(s), cols] += dot_nn(ds, q)
-                dv_ref[krows(s), cols] += dot_nn(p, go_rows)
-                kt = kk.astype(F32).T.astype(BF)
-                return dq + dot_nn(kt, ds)
-
-            dq = lax.fori_loop(0, fr + 1, backward, jnp.zeros((HD, qt_w), F32))
-            dq_ref[qrows, cols] = dq.T.astype(BF)
+                send[slot, h, 0, to, :] = dot_nn(ds, q_ref[:, cols]).astype(BF)
+                send[slot, h, 1, to, :] = dot_nn(p, g_rows[...]).astype(BF)
+                dqt[...] += dot_nn(kk.astype(F32).T.astype(BF), ds)
+                return carry
+
+            lax.fori_loop(0, tiles, step, 0)
+
+        @pl.when(fr >= 2)
+        def _():
+            backward(lax.rem(fr + 2, 4), 0)
+            half_copy(h).start()
+
+        @pl.when(fr == 3)
+        def _():
+            backward(0, 2)
+            if h == 1:
+                add_half(1, 1)
+            full_copy(1, h).start()
+
+        @pl.when(fr >= 1)
+        def _():
+            backward(left, 1)
+
+        if h == 1:
+            @pl.when(fr >= 1)
+            def _():
+                full_copy(0, 1).start()
+
+            @pl.when((fr == 1) | (fr == 2))
+            def _():
+                add_half(0, 0)
+                full_copy(0, 0).start()
+        else:
+            @pl.when(fr == 3)
+            def _():
+                full_copy(0, 0).start()
+
+        backward(fr, 3)
+        dq_ref[:, cols] = dqt[...].T.astype(BF)
+
+    @pl.when(fr == 0)
+    def _():
+        half_copy(1).wait_recv()
+        send[2, 1] = half_in[1]
+        full_copy(1, 1).start()
+
+    def take(side, h):
+        full_copy(side, h).wait_recv()
+        for j in range(2):
+            send[3, h, j] = (send[3, h, j].astype(F32) + full_in[side, h, j].astype(F32)).astype(BF)
+
+    @pl.when(fr <= 2)
+    def _():
+        take(0, 1)
+        take(0, 0)
+
+    @pl.when(fr == 0)
+    def _():
+        take(1, 0)
+
+    @pl.when(fr <= 1)
+    def _():
+        take(1, 1)
+
+    for h in range(2):
+        cols = pl.ds(h * HD, HD)
+        dk_ref[:, cols] = send[3, h, 0]
+        dv_ref[:, cols] = send[3, h, 1]
+
+    for h in range(2):
+        @pl.when(fr >= 2)
+        def _():
+            half_copy(h).wait_send()
+
+        @pl.when(fr >= 1)
+        def _():
+            full_copy(0, h).wait_send()
+
+    @pl.when(fr == 3)
+    def _():
+        full_copy(1, 0).wait_send()
+
+    @pl.when((fr == 3) | (fr == 0))
+    def _():
+        full_copy(1, 1).wait_send()
 
 
 def attention_call(q, k, v, go):
     span, width = q.shape
     vm = pl.BlockSpec(memory_space=pltpu.VMEM)
+    dma = pltpu.SemaphoreType.DMA
     return pl.pallas_call(
         attention_kernel,
-        out_shape=(
-            jax.ShapeDtypeStruct(q.shape, BF),
-            jax.ShapeDtypeStruct(k.shape, F32),
-            jax.ShapeDtypeStruct(v.shape, F32),
-        ),
+        out_shape=(jax.ShapeDtypeStruct(q.shape, BF),) * 3,
         in_specs=[vm] * 4,
         out_specs=(vm,) * 3,
-        scratch_shapes=[pltpu.VMEM((4, span, 512), BF)],
-        compiler_params=pltpu.CompilerParams(vmem_limit_bytes=VMEM_LIMIT),
+        scratch_shapes=[
+            pltpu.VMEM((4 * span, span), BF),
+            pltpu.VMEM((HD, span), BF),
+            pltpu.VMEM((HD, span), BF),
+            pltpu.VMEM((HD, span), BF),
+            pltpu.VMEM((span, HD), BF),
+            pltpu.VMEM((HD, span), F32),
+            pltpu.VMEM((4, 2, 2, span, HD), BF),
+            pltpu.VMEM((2, 2, span, HD), BF),
+            pltpu.VMEM((2, 2, 2, span, HD), BF),
+            dma((2,)), dma((2,)), dma((2, 2)), dma((2, 2)),
+        ],
+        compiler_params=pltpu.CompilerParams(
+            collective_id=1, has_side_effects=True, vmem_limit_bytes=VMEM_LIMIT),
         cost_estimate=pl.CostEstimate(flops=10 * 10**9, bytes_accessed=20 * 10**6, transcendentals=0),
         name="attention",
     )(q, k, v, go)
@@ -478,8 +594,6 @@
         expert_ids.T, gate_weights, out_grad, stored_pre.reshape(toks, -1), hidden_state,
         w_down[0], w_gate[0], w_up[0], queries.shape[1])
     dq, dk, dv = attention_call(queries, key_all, value_all, go)
-    dk = lax.psum_scatter(dk.astype(BF), "frame", scatter_dimension=0, tiled=True)
-    dv = lax.psum_scatter(dv.astype(BF), "frame", scatter_dimension=0, tiled=True)
     return resid, dq, dk, dv
 
 

time: 380 us -> 348 us (0.916)
  waiting for transfers between devices: 86 us -> 1.42 us
  Pallas kernels: 266 us -> 321 us
  other arithmetic: 7.46 us -> 0 us
  local copies, waits for them, and re-layouts: 6.85 us -> 10.7 us
    reduce_scatter x2 -> x0, waiting for transfers between devices: 84.6 us -> none  [the longest x1 52.1 us: on_device(): lax.psum_scatter(dk.astype(BF), 'frame', scatter_dimension=0, tiled=True)]
    pallas_call x1, Pallas kernels: 17.2 us -> 72.6 us  [attention_call(): pl.pallas_call(attention_kernel, out_shape=(jax.ShapeDtypeStruct(q.shape,...]
    convert_element_type x2 -> x0, other arithmetic: 7.46 us -> none  [the longest x1 3.75 us: on_device(): dk.astype(BF)]
    unnamed x4 -> x11, local copies, waits for them, and re-layouts: 2.39 us -> 6.21 us
  transfers between devices with their start and end apart: 4 -> 2, of which waited for: 2 -> 0; matrix products, arithmetic and copies ran while one was open for 3% -> 2% of each run, Pallas kernels for 65% -> 72%
where the time goes in v2:
time: 348 us; the launch traced here: 347 us
  Pallas kernels  321 us (92%)
  between operations  14.1 us (4%)
  local copies, waits for them, and re-layouts  10.7 us (3%)
    pallas_call x1, Pallas kernels, moe_call(): pl.pallas_call(moe_kernel, out_shape=(jax.ShapeDtypeStruct((toks, width),...  249 us
    pallas_call x1, Pallas kernels, attention_call(): pl.pallas_call(attention_kernel, out_shape=(jax.ShapeDtypeStruct(q.shape,...  72.6 us
  transfers between devices with their start and end apart: 2, of which 0 were waited for; matrix products, arithmetic and copies ran while one was open for 2% of the time, Pallas kernels for 72%

profile of v2, /device:TPU:1, one launch (start us, length us, event | category | flops | bytes accessed | tf_op | source)
XLA Modules:
  0.0 347.4 jit_solution(2267922314006894880)
XLA Ops:
  7.2 0.0 all-gather.3.cloned.1.call-start
  7.2 0.7 all-gather.3.cloned.1.call-update
  7.9 0.0 all-gather.5.cloned.1.call-start
  7.9 0.7 all-gather.5.cloned.1.call-update
  8.6 1.4 copy.15.gw_ref
  10.1 4.5 %reshape.11.st_ref = bf16[128,8192]{1,0:T(8,128)(2,1)} reshape(bf16[128,2,2,2048]{3,2,1,0:T(2,128)(2,1)} %param.16) | data formatting | bytes 4194304 | tf_op jit(solution)/shard_map/reshape | solution.py:594
  14.5 248.6 %moe.1 = (bf16[128,4096]{1,0:T(8,128)(2,1)}, bf16[1024,256]{1,0:T(8,128)(2,1)}) custom-call(s32[2,128]{1,0:T(2,128)} %bitcast.7, f32[128,2]{1,0:T(8,128)} %copy.15.gw_ref, bf16[128,4096]{1,0:T(8,128)(2,1)} %og_ref.1, bf16[128,8192]{1,0:T(8,128)(2,1)} %reshape.11.st_ref, bf16[128,4096]{1,0:T(8,128)(2,1)} %hs_ref.1, bf16[512,4096]{1,0:T(8,128)(2,1)} %bitcast.4, ...), custom_call_target="tpu_custom_call" | custom-call | flops 15000000512 | bytes 20000000 | tf_op jit(solution)/shard_map/moe/pallas_call | solution.py:356
  263.1 0.0 all-gather.3.cloned.1.call-done.k_ref
  263.2 0.0 all-gather.5.cloned.1.call-done.v_ref
  263.2 72.6 %attention.1 = (bf16[1024,256]{1,0:T(8,128)(2,1)}, bf16[1024,256]{1,0:T(8,128)(2,1)}, bf16[1024,256]{1,0:T(8,128)(2,1)}) custom-call(bf16[1024,256]{1,0:T(8,128)(2,1)} %q_ref.1, bf16[4096,256]{1,0:T(8,128)(2,1)} %all-gather.3.cloned.1.call-done.k_ref, bf16[4096,256]{1,0:T(8,128)(2,1)} %all-gather.5.cloned.1.call-done.v_ref, ...), custom_call_target="tpu_custom_call" | custom-call | flops 10000000000 | bytes 20000000 | tf_op jit(solution)/shard_map/attention/pallas_call | solution.py:560
  335.8 0.0 copy-start.2
  335.8 0.0 copy-start.1
  335.8 0.0 copy-start
  335.8 2.4 copy.20
  338.2 0.0 copy-done.2
  338.2 0.8 copy.21
  339.0 0.0 copy-done.1
  339.0 0.8 copy.22
  339.8 0.0 copy-done
  339.8 0.8 copy.23
Async XLA Ops:
  7.2 256.0 %all-gather.3.cloned.1.call-start = ((), (), s32[]{:S(2)}) async-start(), calls=%async_computation | async-start | bytes 2621440 | tf_op jit(solution)/shard_map/all_gather | solution.py:590
  7.9 255.3 %all-gather.5.cloned.1.call-start = ((), (), s32[]{:S(2)}) async-start(), calls=%async_computation.1 | async-start | bytes 2621440 | tf_op jit(solution)/shard_map/all_gather | solution.py:591
  335.8 2.4 copy-start.2
  335.8 3.2 copy-start.1
  335.8 4.0 %copy-start = (bf16[1024,256]{1,0:T(8,128)(2,1)S(1)}, bf16[1024,256]{1,0:T(8,128)(2,1)}, u32[]{:S(2)}) copy-start(bf16[1024,256]{1,0:T(8,128)(2,1)} %get-tuple-element.21) | copy-start | bytes 1572868
Sparse Core Ops, SparseCore 0:
  9.7 42.8 all-gather.2
  54.2 49.3 all-gather.4
